TPU v7x, 32 devices: a whole 2x2x4 slice. The times are simulated.
32 devices in a mesh: frame: 16 (over z, x, core), group: 2 (over y).
Axes of the slice: x: 2, y: 2, z: 4, core: 2. Of those that a mesh axis runs over, the one named last changes fastest.
Arguments:
- queries: bfloat16 [2048, 2048], P('frame', 'group'), may hold values from -6 to 6
- keys: bfloat16 [2048, 256], P('frame', 'group'), may hold values from -50 to 50
- values: bfloat16 [2048, 256], P('frame', 'group'), may hold values from -6 to 6
- q_gain: float32 [128], replicated, may hold values from 0.4 to 2.5
- frame_bounds: int32 [2, 2048], P(None, 'frame'), may hold values from 0 to 16, as said below
- output_weight: bfloat16 [2, 1024, 4096], P('group', 'frame'), may hold values from -0.25 to 0.25
- attn_gate: float32 [1], replicated, may hold values from 0.4 to 1.6
Outputs:
- projected: bfloat16 [2048, 4096], P('frame', 'group')
Inputs may be any that keep to these rules, and one draw needn't show every extreme that they name: `frame_bounds`: row 0 is below row 1 for every text token.
All inputs are finite; a program needn't handle non-finite values.
Results may differ from a plain program's by a relative error of at most 0.008.
The roundings to bfloat16 on the way count: a program that leaves them out, or rounds other values in their place, can miss the bound.
Values may be sent and summed in bfloat16 or wider, within the bound.
A program may use at most 64 MiB of HBM per device.

v0:
```python
import math

import jax
import jax.numpy as jnp
from jax import lax
from jax.sharding import PartitionSpec as P

HEAD_WIDTH = 128
V_DEV = 128


very_low = -1e30


def from_behind(value, axis, steps):
    count = lax.axis_size(axis)
    pairs = [(source, (source + steps) % count) for source in range(count)]
    return lax.ppermute(value, axis, pairs)


def absorb(carry_state, kv_block, first_row, normalized_input, lower_rows, upper_rows):
    run_max, run_sum, run_out = carry_state
    key_count = kv_block.shape[1]
    scores = jnp.einsum(
        "rd,kd->rk", normalized_input, kv_block[0], preferred_element_type=jnp.float32
    )
    scores = scores * (1.0 / math.sqrt(kv_block.shape[2]))
    block_ids = (first_row + lax.iota(jnp.int32, key_count)) // V_DEV
    allowed = (block_ids[None, :] >= lower_rows) & (block_ids[None, :] < upper_rows)
    masked = jnp.where(allowed, scores, very_low)
    newest = jnp.maximum(run_max, jnp.max(masked, axis=1, keepdims=True))
    weights = jnp.where(allowed, jnp.exp(masked - newest), 0.0)
    factor = jnp.exp(run_max - newest)
    run_sum = run_sum * factor + jnp.sum(weights, axis=1, keepdims=True)
    run_out = run_out * factor + jnp.dot(
        weights.astype(jnp.bfloat16), kv_block[1], preferred_element_type=jnp.float32
    )
    return (newest, run_sum, run_out)


def local(queries, keys, values, q_gain, frame_bounds, output_weight, attn_gate):
    rows_tok = queries.shape[0]
    width = queries.shape[1]
    heads_here = width // HEAD_WIDTH
    as_float = queries.astype(jnp.float32).reshape(rows_tok * heads_here, HEAD_WIDTH)
    normalized_input = (
        as_float * lax.rsqrt(jnp.mean(as_float * as_float, axis=-1, keepdims=True) + 1e-05) * q_gain
    )
    normalized_input = normalized_input.astype(jnp.bfloat16)
    lower_rows = jnp.repeat(frame_bounds[0], heads_here)[:, None]
    upper_rows = jnp.repeat(frame_bounds[1], heads_here)[:, None]
    stacked = jnp.stack([keys, values])
    frames = lax.axis_size("frame")
    own_index = lax.axis_index("frame")
    row_total = rows_tok * heads_here
    initial = (
        jnp.full((row_total, 1), very_low, jnp.float32),
        jnp.zeros((row_total, 1), jnp.float32),
        jnp.zeros((row_total, HEAD_WIDTH), jnp.float32),
    )

    def visit(carry_state, kv_block, anchor):
        return absorb(
            carry_state, kv_block, anchor * V_DEV, normalized_input, lower_rows, upper_rows
        )

    carry_state = visit(initial, stacked, own_index)
    half_loop = frames // 2

    def step_two(i, carry):
        state_now, ahead_kv, behind = carry
        ahead_kv = from_behind(ahead_kv, "frame", 1)
        behind = from_behind(behind, "frame", -1)
        state_now = visit(state_now, ahead_kv, (own_index - i) % frames)
        back_anchor = jnp.where(i == half_loop, -1, (own_index + i) % frames)
        state_now = visit(state_now, behind, back_anchor)
        return (state_now, ahead_kv, behind)

    carry_state, unused_ahead, unused_behind = lax.fori_loop(
        1, half_loop + 1, step_two, (carry_state, stacked, stacked)
    )
    run_max, run_sum, run_out = carry_state
    attended = (run_out / run_sum).astype(jnp.bfloat16).reshape(rows_tok, width)
    gate_value = jnp.tanh(attn_gate[0])
    summed = jnp.dot(
        attended,
        lax.all_gather(output_weight, "frame", axis=1, tiled=True)[0],
        preferred_element_type=jnp.float32,
    )
    combined = lax.psum_scatter(summed, "group", scatter_dimension=1, tiled=True)
    return (gate_value * combined).astype(jnp.bfloat16)


def solution(mesh):
    placed = (
        P("frame", "group"),
        P("frame", "group"),
        P("frame", "group"),
        P(),
        P(None, "frame"),
        P("group", "frame", None),
        P(),
    )
    return jax.shard_map(
        local, mesh=mesh, in_specs=placed, out_specs=P("frame", "group"), check_vma=False
    )
```

profile of v0, /device:TPU:0, one launch (start us, length us, event | category | flops | bytes accessed | tf_op | source)
XLA Modules:
  0.0 139.7 jit_solution(11748960651995025045)
XLA Ops:
  6.5 0.7 all-gather.2.cloned.1.call-update
  7.3 0.8 slice_bitcast_fusion.9
  8.4 1.1 reshape.118
  9.7 0.9 multiply_convert_fusion.1
  10.6 0.8 pad_maximum_fusion
  11.4 1.0 fusion.42
  12.6 1.1 convolution_add_fusion.1
  13.8 81.0 %while.25 = (s32[]{:T(128)}, f32[1024,1]{0,1:T(1,128)S(1)}, f32[1024,1]{0,1:T(1,128)S(1)}, f32[1024,128]{1,0:T(8,128)S(1)}, bf16[2,128,128]{2,1,0:T(8,128)(2,1)S...) while((s32[]{:T(128)}, f32[1024,1]{0,1:T(1,128)S(1)}, ...), condition=%wide.region_8.9_spmd.clone, body=%wide.region_3.8_spmd.clone.sunk | while | flops 139468832 | bytes 6862357 | solution.py:79
  13.8 5.5 %collective-permute-start = (bf16[2,128,128]{2,1,0:T(8,128)(2,1)S(1)}, bf16[2,128,128]{2,1,0:T(8,128)(2,1)S(1)}, u32[]{:S(2)}, u32[]{:S(2)}) collective-permute-start(bf16[2,128,128]{2,1,0:T(8,128)(2,1)S(1)} %get-tuple-element.458), channel_id=1, source_target_pairs={{0,30},{2,0},{4,2},{6,4},{8,6},{10,8},{12,10},{14,12},{16,14},{18,... | collective-permute-start | bytes 196616 | tf_op jit(solution)/shard_map/while/body/eval_jaxpr/ppermute | solution.py:18
  19.7 1.5 %collective-permute-done = bf16[2,128,128]{2,1,0:T(8,128)(2,1)S(1)} collective-permute-done((bf16[2,128,128]{2,1,0:T(8,128)(2,1)S(1)}, bf16[2,128,128]{2,1,0:T(8,128)(2,1)S(1)}, u32[]{:S(2)}, u32[]{:S(2)}) %collective-permute-start) | collective-permute-done | bytes 65568 | tf_op jit(solution)/shard_map/while/body/eval_jaxpr/ppermute | solution.py:18
  21.5 4.4 %collective-permute-done.1 = bf16[2,128,128]{2,1,0:T(8,128)(2,1)S(1)} collective-permute-done((bf16[2,128,128]{2,1,0:T(8,128)(2,1)S(1)}, bf16[2,128,128]{2,1,0:T(8,128)(2,1)S(1)}, u32[]{:S(2)}, u32[]{:S(2)}) %collective-permute-start.1) | collective-permute-done | bytes 65568 | tf_op jit(solution)/shard_map/while/body/eval_jaxpr/ppermute | solution.py:18
  26.5 0.3 fusion.67
  26.9 0.7 fusion.68
  27.8 0.4 collective-permute-start.1
  28.6 2.3 %collective-permute-done = bf16[2,128,128]{2,1,0:T(8,128)(2,1)S(1)} collective-permute-done((bf16[2,128,128]{2,1,0:T(8,128)(2,1)S(1)}, bf16[2,128,128]{2,1,0:T(8,128)(2,1)S(1)}, u32[]{:S(2)}, u32[]{:S(2)}) %collective-permute-start) | collective-permute-done | bytes 65568 | tf_op jit(solution)/shard_map/while/body/eval_jaxpr/ppermute | solution.py:18
  31.2 4.4 %collective-permute-done.1 = bf16[2,128,128]{2,1,0:T(8,128)(2,1)S(1)} collective-permute-done((bf16[2,128,128]{2,1,0:T(8,128)(2,1)S(1)}, bf16[2,128,128]{2,1,0:T(8,128)(2,1)S(1)}, u32[]{:S(2)}, u32[]{:S(2)}) %collective-permute-start.1) | collective-permute-done | bytes 65568 | tf_op jit(solution)/shard_map/while/body/eval_jaxpr/ppermute | solution.py:18
  36.2 0.3 fusion.67
  36.6 0.7 fusion.68
  37.3 0.3 collective-permute-start
  38.2 1.3 collective-permute-done
  39.8 4.5 %collective-permute-done.1 = bf16[2,128,128]{2,1,0:T(8,128)(2,1)S(1)} collective-permute-done((bf16[2,128,128]{2,1,0:T(8,128)(2,1)S(1)}, bf16[2,128,128]{2,1,0:T(8,128)(2,1)S(1)}, u32[]{:S(2)}, u32[]{:S(2)}) %collective-permute-start.1) | collective-permute-done | bytes 65568 | tf_op jit(solution)/shard_map/while/body/eval_jaxpr/ppermute | solution.py:18
  45.0 0.3 fusion.67
  45.4 0.7 fusion.68
  46.2 0.5 collective-permute-start.1
  47.0 2.4 %collective-permute-done = bf16[2,128,128]{2,1,0:T(8,128)(2,1)S(1)} collective-permute-done((bf16[2,128,128]{2,1,0:T(8,128)(2,1)S(1)}, bf16[2,128,128]{2,1,0:T(8,128)(2,1)S(1)}, u32[]{:S(2)}, u32[]{:S(2)}) %collective-permute-start) | collective-permute-done | bytes 65568 | tf_op jit(solution)/shard_map/while/body/eval_jaxpr/ppermute | solution.py:18
  49.7 3.8 %collective-permute-done.1 = bf16[2,128,128]{2,1,0:T(8,128)(2,1)S(1)} collective-permute-done((bf16[2,128,128]{2,1,0:T(8,128)(2,1)S(1)}, bf16[2,128,128]{2,1,0:T(8,128)(2,1)S(1)}, u32[]{:S(2)}, u32[]{:S(2)}) %collective-permute-start.1) | collective-permute-done | bytes 65568 | tf_op jit(solution)/shard_map/while/body/eval_jaxpr/ppermute | solution.py:18
  54.1 0.3 fusion.67
  54.5 0.7 fusion.68
  55.2 0.9 collective-permute-start
  56.6 2.8 %collective-permute-done = bf16[2,128,128]{2,1,0:T(8,128)(2,1)S(1)} collective-permute-done((bf16[2,128,128]{2,1,0:T(8,128)(2,1)S(1)}, bf16[2,128,128]{2,1,0:T(8,128)(2,1)S(1)}, u32[]{:S(2)}, u32[]{:S(2)}) %collective-permute-start) | collective-permute-done | bytes 65568 | tf_op jit(solution)/shard_map/while/body/eval_jaxpr/ppermute | solution.py:18
  59.7 4.4 %collective-permute-done.1 = bf16[2,128,128]{2,1,0:T(8,128)(2,1)S(1)} collective-permute-done((bf16[2,128,128]{2,1,0:T(8,128)(2,1)S(1)}, bf16[2,128,128]{2,1,0:T(8,128)(2,1)S(1)}, u32[]{:S(2)}, u32[]{:S(2)}) %collective-permute-start.1) | collective-permute-done | bytes 65568 | tf_op jit(solution)/shard_map/while/body/eval_jaxpr/ppermute | solution.py:18
  65.1 0.7 fusion.68
  65.8 0.3 collective-permute-start
  66.7 2.6 %collective-permute-done = bf16[2,128,128]{2,1,0:T(8,128)(2,1)S(1)} collective-permute-done((bf16[2,128,128]{2,1,0:T(8,128)(2,1)S(1)}, bf16[2,128,128]{2,1,0:T(8,128)(2,1)S(1)}, u32[]{:S(2)}, u32[]{:S(2)}) %collective-permute-start) | collective-permute-done | bytes 65568 | tf_op jit(solution)/shard_map/while/body/eval_jaxpr/ppermute | solution.py:18
  69.6 4.4 %collective-permute-done.1 = bf16[2,128,128]{2,1,0:T(8,128)(2,1)S(1)} collective-permute-done((bf16[2,128,128]{2,1,0:T(8,128)(2,1)S(1)}, bf16[2,128,128]{2,1,0:T(8,128)(2,1)S(1)}, u32[]{:S(2)}, u32[]{:S(2)}) %collective-permute-start.1) | collective-permute-done | bytes 65568 | tf_op jit(solution)/shard_map/while/body/eval_jaxpr/ppermute | solution.py:18
  75.0 0.7 fusion.68
  76.7 2.3 %collective-permute-done = bf16[2,128,128]{2,1,0:T(8,128)(2,1)S(1)} collective-permute-done((bf16[2,128,128]{2,1,0:T(8,128)(2,1)S(1)}, bf16[2,128,128]{2,1,0:T(8,128)(2,1)S(1)}, u32[]{:S(2)}, u32[]{:S(2)}) %collective-permute-start) | collective-permute-done | bytes 65568 | tf_op jit(solution)/shard_map/while/body/eval_jaxpr/ppermute | solution.py:18
  79.2 4.3 %collective-permute-done.1 = bf16[2,128,128]{2,1,0:T(8,128)(2,1)S(1)} collective-permute-done((bf16[2,128,128]{2,1,0:T(8,128)(2,1)S(1)}, bf16[2,128,128]{2,1,0:T(8,128)(2,1)S(1)}, u32[]{:S(2)}, u32[]{:S(2)}) %collective-permute-start.1) | collective-permute-done | bytes 65568 | tf_op jit(solution)/shard_map/while/body/eval_jaxpr/ppermute | solution.py:18
  84.1 0.3 fusion.67
  84.5 0.7 fusion.68
  85.2 0.4 collective-permute-start
  86.2 2.4 %collective-permute-done = bf16[2,128,128]{2,1,0:T(8,128)(2,1)S(1)} collective-permute-done((bf16[2,128,128]{2,1,0:T(8,128)(2,1)S(1)}, bf16[2,128,128]{2,1,0:T(8,128)(2,1)S(1)}, u32[]{:S(2)}, u32[]{:S(2)}) %collective-permute-start) | collective-permute-done | bytes 65568 | tf_op jit(solution)/shard_map/while/body/eval_jaxpr/ppermute | solution.py:18
  88.8 4.2 %collective-permute-done.1 = bf16[2,128,128]{2,1,0:T(8,128)(2,1)S(1)} collective-permute-done((bf16[2,128,128]{2,1,0:T(8,128)(2,1)S(1)}, bf16[2,128,128]{2,1,0:T(8,128)(2,1)S(1)}, u32[]{:S(2)}, u32[]{:S(2)}) %collective-permute-start.1) | collective-permute-done | bytes 65568 | tf_op jit(solution)/shard_map/while/body/eval_jaxpr/ppermute | solution.py:18
  93.7 0.3 fusion.67
  94.1 0.7 fusion.68
  95.2 6.0 %fusion.27 = f32[128,4096]{1,0:T(8,128)} fusion(bf16[128,1024]{1,0:T(8,128)(2,1)S(1)} %reshape.116, bf16[1,1024,4096]{2,1,0:T(8,128)(2,1)} %all-gather.2.cloned.1.call-done), kind=kOutput, calls=%fused_computation.45 | convolution fusion | flops 1073741824 | bytes 10747904 | tf_op jit(solution)/shard_map/dot_general | solution.py:85
  101.9 28.8 %reduce-scatter.2.cloned.1.call-done = f32[128,2048]{1,0:T(8,128)} async-done(((f32[128,4096]{1,0:T(8,128)}), f32[128,2048]{1,0:T(8,128)}) %reduce-scatter.2.cloned.1.call-update) | async-done | bytes 1048592 | tf_op jit(solution)/shard_map/reduce_scatter | solution.py:90
  130.7 2.1 %multiply_convert_fusion = bf16[128,2048]{1,0:T(8,128)(2,1)} fusion(f32[128,2048]{1,0:T(8,128)} %reduce-scatter.2.cloned.1.call-done, f32[]{:T(128)} %bitcast), kind=kLoop, calls=%fused_computation.50 | loop fusion | flops 524288 | bytes 1572868 | tf_op jit(solution)/shard_map/convert_element_type | solution.py:91
  (132 shorter events, 13.4 us)
Async XLA Ops:
  6.5 88.6 %all-gather.2.cloned.1.call-start = ((), (), s32[]{:S(2)}) async-start(), calls=%async_computation.1 | async-start | bytes 8912896 | tf_op jit(solution)/shard_map/all_gather | solution.py:87
  7.3 123.5 %reduce-scatter.2.cloned.1.call-start = ((), (), s32[]{:S(2)}) async-start(), calls=%async_computation.2 | async-start | bytes 3145728 | tf_op jit(solution)/shard_map/reduce_scatter | solution.py:90
  13.8 7.4 %collective-permute-start = (bf16[2,128,128]{2,1,0:T(8,128)(2,1)S(1)}, bf16[2,128,128]{2,1,0:T(8,128)(2,1)S(1)}, u32[]{:S(2)}, u32[]{:S(2)}) collective-permute-start(bf16[2,128,128]{2,1,0:T(8,128)(2,1)S(1)} %get-tuple-element.458), channel_id=1, source_target_pairs={{0,30},{2,0},{4,2},{6,4},{8,6},{10,8},{12,10},{14,12},{16,14},{18,... | collective-permute-start | bytes 196616 | tf_op jit(solution)/shard_map/while/body/eval_jaxpr/ppermute | solution.py:18
  19.3 6.6 %collective-permute-start.1 = (bf16[2,128,128]{2,1,0:T(8,128)(2,1)S(1)}, bf16[2,128,128]{2,1,0:T(8,128)(2,1)S(1)}, u32[]{:S(2)}, u32[]{:S(2)}) collective-permute-start(bf16[2,128,128]{2,1,0:T(8,128)(2,1)S(1)} %get-tuple-element.457), channel_id=1, source_target_pairs={{0,2},{2,4},{4,6},{6,8},{8,10},{10,12},{12,14},{14,16},{16,18},{18... | collective-permute-start | bytes 196616 | tf_op jit(solution)/shard_map/while/body/eval_jaxpr/ppermute | solution.py:18
  27.6 3.3 %collective-permute-start = (bf16[2,128,128]{2,1,0:T(8,128)(2,1)S(1)}, bf16[2,128,128]{2,1,0:T(8,128)(2,1)S(1)}, u32[]{:S(2)}, u32[]{:S(2)}) collective-permute-start(bf16[2,128,128]{2,1,0:T(8,128)(2,1)S(1)} %get-tuple-element.458), channel_id=1, source_target_pairs={{0,30},{2,0},{4,2},{6,4},{8,6},{10,8},{12,10},{14,12},{16,14},{18,... | collective-permute-start | bytes 196616 | tf_op jit(solution)/shard_map/while/body/eval_jaxpr/ppermute | solution.py:18
  27.8 7.8 %collective-permute-start.1 = (bf16[2,128,128]{2,1,0:T(8,128)(2,1)S(1)}, bf16[2,128,128]{2,1,0:T(8,128)(2,1)S(1)}, u32[]{:S(2)}, u32[]{:S(2)}) collective-permute-start(bf16[2,128,128]{2,1,0:T(8,128)(2,1)S(1)} %get-tuple-element.457), channel_id=1, source_target_pairs={{0,2},{2,4},{4,6},{6,8},{8,10},{10,12},{12,14},{14,16},{16,18},{18... | collective-permute-start | bytes 196616 | tf_op jit(solution)/shard_map/while/body/eval_jaxpr/ppermute | solution.py:18
  37.3 2.3 %collective-permute-start = (bf16[2,128,128]{2,1,0:T(8,128)(2,1)S(1)}, bf16[2,128,128]{2,1,0:T(8,128)(2,1)S(1)}, u32[]{:S(2)}, u32[]{:S(2)}) collective-permute-start(bf16[2,128,128]{2,1,0:T(8,128)(2,1)S(1)} %get-tuple-element.458), channel_id=1, source_target_pairs={{0,30},{2,0},{4,2},{6,4},{8,6},{10,8},{12,10},{14,12},{16,14},{18,... | collective-permute-start | bytes 196616 | tf_op jit(solution)/shard_map/while/body/eval_jaxpr/ppermute | solution.py:18
  37.7 6.7 %collective-permute-start.1 = (bf16[2,128,128]{2,1,0:T(8,128)(2,1)S(1)}, bf16[2,128,128]{2,1,0:T(8,128)(2,1)S(1)}, u32[]{:S(2)}, u32[]{:S(2)}) collective-permute-start(bf16[2,128,128]{2,1,0:T(8,128)(2,1)S(1)} %get-tuple-element.457), channel_id=1, source_target_pairs={{0,2},{2,4},{4,6},{6,8},{8,10},{10,12},{12,14},{14,16},{16,18},{18... | collective-permute-start | bytes 196616 | tf_op jit(solution)/shard_map/while/body/eval_jaxpr/ppermute | solution.py:18
  46.1 3.3 %collective-permute-start = (bf16[2,128,128]{2,1,0:T(8,128)(2,1)S(1)}, bf16[2,128,128]{2,1,0:T(8,128)(2,1)S(1)}, u32[]{:S(2)}, u32[]{:S(2)}) collective-permute-start(bf16[2,128,128]{2,1,0:T(8,128)(2,1)S(1)} %get-tuple-element.458), channel_id=1, source_target_pairs={{0,30},{2,0},{4,2},{6,4},{8,6},{10,8},{12,10},{14,12},{16,14},{18,... | collective-permute-start | bytes 196616 | tf_op jit(solution)/shard_map/while/body/eval_jaxpr/ppermute | solution.py:18
  46.2 7.3 %collective-permute-start.1 = (bf16[2,128,128]{2,1,0:T(8,128)(2,1)S(1)}, bf16[2,128,128]{2,1,0:T(8,128)(2,1)S(1)}, u32[]{:S(2)}, u32[]{:S(2)}) collective-permute-start(bf16[2,128,128]{2,1,0:T(8,128)(2,1)S(1)} %get-tuple-element.457), channel_id=1, source_target_pairs={{0,2},{2,4},{4,6},{6,8},{8,10},{10,12},{12,14},{14,16},{16,18},{18... | collective-permute-start | bytes 196616 | tf_op jit(solution)/shard_map/while/body/eval_jaxpr/ppermute | solution.py:18
  55.2 4.1 %collective-permute-start = (bf16[2,128,128]{2,1,0:T(8,128)(2,1)S(1)}, bf16[2,128,128]{2,1,0:T(8,128)(2,1)S(1)}, u32[]{:S(2)}, u32[]{:S(2)}) collective-permute-start(bf16[2,128,128]{2,1,0:T(8,128)(2,1)S(1)} %get-tuple-element.458), channel_id=1, source_target_pairs={{0,30},{2,0},{4,2},{6,4},{8,6},{10,8},{12,10},{14,12},{16,14},{18,... | collective-permute-start | bytes 196616 | tf_op jit(solution)/shard_map/while/body/eval_jaxpr/ppermute | solution.py:18
  56.2 7.9 %collective-permute-start.1 = (bf16[2,128,128]{2,1,0:T(8,128)(2,1)S(1)}, bf16[2,128,128]{2,1,0:T(8,128)(2,1)S(1)}, u32[]{:S(2)}, u32[]{:S(2)}) collective-permute-start(bf16[2,128,128]{2,1,0:T(8,128)(2,1)S(1)} %get-tuple-element.457), channel_id=1, source_target_pairs={{0,2},{2,4},{4,6},{6,8},{8,10},{10,12},{12,14},{14,16},{16,18},{18... | collective-permute-start | bytes 196616 | tf_op jit(solution)/shard_map/while/body/eval_jaxpr/ppermute | solution.py:18
  65.8 3.5 %collective-permute-start = (bf16[2,128,128]{2,1,0:T(8,128)(2,1)S(1)}, bf16[2,128,128]{2,1,0:T(8,128)(2,1)S(1)}, u32[]{:S(2)}, u32[]{:S(2)}) collective-permute-start(bf16[2,128,128]{2,1,0:T(8,128)(2,1)S(1)} %get-tuple-element.458), channel_id=1, source_target_pairs={{0,30},{2,0},{4,2},{6,4},{8,6},{10,8},{12,10},{14,12},{16,14},{18,... | collective-permute-start | bytes 196616 | tf_op jit(solution)/shard_map/while/body/eval_jaxpr/ppermute | solution.py:18
  66.1 7.8 %collective-permute-start.1 = (bf16[2,128,128]{2,1,0:T(8,128)(2,1)S(1)}, bf16[2,128,128]{2,1,0:T(8,128)(2,1)S(1)}, u32[]{:S(2)}, u32[]{:S(2)}) collective-permute-start(bf16[2,128,128]{2,1,0:T(8,128)(2,1)S(1)} %get-tuple-element.457), channel_id=1, source_target_pairs={{0,2},{2,4},{4,6},{6,8},{8,10},{10,12},{12,14},{14,16},{16,18},{18... | collective-permute-start | bytes 196616 | tf_op jit(solution)/shard_map/while/body/eval_jaxpr/ppermute | solution.py:18
  75.7 3.2 %collective-permute-start = (bf16[2,128,128]{2,1,0:T(8,128)(2,1)S(1)}, bf16[2,128,128]{2,1,0:T(8,128)(2,1)S(1)}, u32[]{:S(2)}, u32[]{:S(2)}) collective-permute-start(bf16[2,128,128]{2,1,0:T(8,128)(2,1)S(1)} %get-tuple-element.458), channel_id=1, source_target_pairs={{0,30},{2,0},{4,2},{6,4},{8,6},{10,8},{12,10},{14,12},{16,14},{18,... | collective-permute-start | bytes 196616 | tf_op jit(solution)/shard_map/while/body/eval_jaxpr/ppermute | solution.py:18
  76.0 7.5 %collective-permute-start.1 = (bf16[2,128,128]{2,1,0:T(8,128)(2,1)S(1)}, bf16[2,128,128]{2,1,0:T(8,128)(2,1)S(1)}, u32[]{:S(2)}, u32[]{:S(2)}) collective-permute-start(bf16[2,128,128]{2,1,0:T(8,128)(2,1)S(1)} %get-tuple-element.457), channel_id=1, source_target_pairs={{0,2},{2,4},{4,6},{6,8},{8,10},{10,12},{12,14},{14,16},{16,18},{18... | collective-permute-start | bytes 196616 | tf_op jit(solution)/shard_map/while/body/eval_jaxpr/ppermute | solution.py:18
  85.2 3.3 %collective-permute-start = (bf16[2,128,128]{2,1,0:T(8,128)(2,1)S(1)}, bf16[2,128,128]{2,1,0:T(8,128)(2,1)S(1)}, u32[]{:S(2)}, u32[]{:S(2)}) collective-permute-start(bf16[2,128,128]{2,1,0:T(8,128)(2,1)S(1)} %get-tuple-element.458), channel_id=1, source_target_pairs={{0,30},{2,0},{4,2},{6,4},{8,6},{10,8},{12,10},{14,12},{16,14},{18,... | collective-permute-start | bytes 196616 | tf_op jit(solution)/shard_map/while/body/eval_jaxpr/ppermute | solution.py:18
  85.6 7.4 %collective-permute-start.1 = (bf16[2,128,128]{2,1,0:T(8,128)(2,1)S(1)}, bf16[2,128,128]{2,1,0:T(8,128)(2,1)S(1)}, u32[]{:S(2)}, u32[]{:S(2)}) collective-permute-start(bf16[2,128,128]{2,1,0:T(8,128)(2,1)S(1)} %get-tuple-element.457), channel_id=1, source_target_pairs={{0,2},{2,4},{4,6},{6,8},{8,10},{10,12},{12,14},{14,16},{16,18},{18... | collective-permute-start | bytes 196616 | tf_op jit(solution)/shard_map/while/body/eval_jaxpr/ppermute | solution.py:18
Sparse Core Ops, SparseCore 0:
  9.5 84.1 all-gather.1
  101.4 29.3 reduce-scatter.1
where the time goes:
time: 140 us
  waiting for transfers between devices  81.5 us (58%)
  matrix products  20.9 us (15%)
  between operations  14.2 us (10%)
  starting transfers between devices  9.83 us (7%)
  other arithmetic  7.37 us (5%)
  local copies, waits for them, and re-layouts  5.15 us (4%)
    ppermute x16, waiting for transfers between devices, from_behind(): return lax.ppermute(value, axis, pairs)  51.9 us
    reduce_scatter x1, waiting for transfers between devices, local(): lax.psum_scatter(summed, 'group', scatter_dimension=1, tiled=True)  28.8 us
    ppermute x16, starting transfers between devices, from_behind(): return lax.ppermute(value, axis, pairs)  9.79 us
    dot_general x17, matrix products, absorb(): jnp.dot(weights.astype(jnp.bfloat16), kv_block[1], preferred_element_type...  9.57 us
    dot_general x1, matrix products, local(): jnp.dot(attended, lax.all_gather(output_weight, 'frame', axis=1, tiled=Tr...  6.04 us
    dot_general x17, matrix products, absorb(): jnp.einsum('rd,kd->rk', normalized_input, kv_block[0], preferred_element_...  5.28 us
  transfers between devices with their start and end apart: 18, of which 17 were waited for; matrix products, arithmetic and copies ran while one was open for 18% of the time, Pallas kernels for 0%

commit v1 on v0

v1 whole, which is shorter than its diff:
```python
import functools
import math

import jax
import jax.numpy as jnp
from jax import lax
from jax.experimental import pallas as pl
from jax.experimental.pallas import tpu as pltpu
from jax.sharding import PartitionSpec as P

HEAD_WIDTH = 128
V_DEV = 128
INNER = 4
MESH = pl.DeviceIdType.MESH
very_low = -1e30


def kernel(
    frames,
    groups,
    q_ref,
    k_ref,
    v_ref,
    gain_ref,
    bounds_ref,
    w_ref,
    gate_ref,
    out_ref,
    kv,
    att,
    wbuf,
    obuf,
    kv_recv,
    kv_send,
    w_recv,
    w_send,
    wz_recv,
    wz_send,
    att_recv,
    att_send,
    out_recv,
    out_send,
    own_sem,
):
    depth = frames // INNER
    cols = wbuf.shape[4]
    tokens = q_ref.shape[0]
    heads = q_ref.shape[1] // HEAD_WIDTH
    f = lax.axis_index("frame")
    g = lax.axis_index("group")
    z = f // INNER
    a = f % INNER
    xb = a // 2
    cb = a % 2
    a_x = (1 - xb) * 2 + cb
    a_c = xb * 2 + (1 - cb)
    a_xc = (1 - xb) * 2 + (1 - cb)

    barrier = pltpu.get_barrier_semaphore()
    greeted = 0
    for step in range(1, frames):
        pl.semaphore_signal(
            barrier, inc=1, device_id=((f + step) % frames, g), device_id_type=MESH
        )
        greeted += 1
    for dg in range(1, groups):
        for da in range(INNER):
            pl.semaphore_signal(
                barrier,
                inc=1,
                device_id=(z * INNER + (a + da) % INNER, (g + dg) % groups),
                device_id_type=MESH,
            )
            greeted += 1
    kv[z, a, 0] = k_ref[...]
    kv[z, a, 1] = v_ref[...]
    pl.semaphore_wait(barrier, greeted)

    pending = []

    def send(src, dst, send_sem, recv_sem, to):
        copy = pltpu.make_async_remote_copy(
            src_ref=src,
            dst_ref=dst,
            send_sem=send_sem,
            recv_sem=recv_sem,
            device_id=to,
            device_id_type=MESH,
        )
        copy.start()
        pending.append(copy)

    def arrived(slot, send_sem, recv_sem):
        pltpu.make_async_remote_copy(
            src_ref=slot,
            dst_ref=slot,
            send_sem=send_sem,
            recv_sem=recv_sem,
            device_id=(z * INNER + a_x, g),
            device_id_type=MESH,
        ).wait_recv()

    n_kv = 0
    for dz in range(1, depth):
        send(
            kv.at[z, a],
            kv.at[z, a],
            kv_send.at[n_kv],
            kv_recv.at[z, a],
            ((z + dz) % depth * INNER + a, g),
        )
        n_kv += 1

    def columns(ga, aa):
        return pl.ds(pl.multiple_of((ga * INNER + aa) * cols, 128), cols)

    own = pltpu.make_async_copy(w_ref.at[0, :, columns(g, a)], wbuf.at[z, g, a], own_sem)
    own.start()
    n_w = 0
    for dg in range(groups):
        for da in range(INNER):
            if dg == 0 and da == 0:
                continue
            gg = (g + dg) % groups
            aa = (a + da) % INNER
            send(
                w_ref.at[0, :, columns(gg, aa)],
                wbuf.at[z, g, a],
                w_send.at[n_w],
                w_recv.at[g, a],
                (z * INNER + aa, gg),
            )
            n_w += 1

    for dz in range(depth):
        zz = (z + dz) % depth
        if dz:
            arrived(kv.at[zz, a], kv_send.at[0], kv_recv.at[zz, a])
        for aa in (a_x, a_c):
            send(
                kv.at[zz, a],
                kv.at[zz, a],
                kv_send.at[n_kv],
                kv_recv.at[zz, a],
                (z * INNER + aa, g),
            )
            n_kv += 1

    own.wait()
    n_wz = 0
    for dg in range(groups):
        gg = (g + dg) % groups
        for da in range(INNER):
            if dg == 0 and da == 0:
                continue
            aa = (a + da) % INNER
            arrived(wbuf.at[z, gg, aa], w_send.at[0], w_recv.at[gg, aa])
        for dz in range(1, depth):
            send(
                wbuf.at[z, gg],
                wbuf.at[z, gg],
                wz_send.at[n_wz],
                wz_recv.at[z, gg],
                ((z + dz) % depth * INNER + a, g),
            )
            n_wz += 1

    for dz in range(depth):
        zz = (z + dz) % depth
        arrived(kv.at[zz, a_x], kv_send.at[0], kv_recv.at[zz, a_x])
        send(
            kv.at[zz, a_x],
            kv.at[zz, a_x],
            kv_send.at[n_kv],
            kv_recv.at[zz, a_x],
            (z * INNER + a_c, g),
        )
        n_kv += 1
    for dz in range(depth):
        zz = (z + dz) % depth
        for aa in (a_c, a_xc):
            arrived(kv.at[zz, aa], kv_send.at[0], kv_recv.at[zz, aa])

    def spread(row):
        wide = jnp.broadcast_to(bounds_ref[row : row + 1, :].astype(jnp.float32), (tokens, tokens))
        return wide.T[:, :1].astype(jnp.int32)

    low = spread(0)
    high = spread(1)
    scale = 1.0 / math.sqrt(HEAD_WIDTH)
    chunk = INNER * V_DEV

    def one_head(h, carry):
        lanes = pl.ds(pl.multiple_of(h * HEAD_WIDTH, HEAD_WIDTH), HEAD_WIDTH)
        x = q_ref[:, lanes].astype(jnp.float32)
        x = x * lax.rsqrt(jnp.mean(x * x, axis=-1, keepdims=True) + 1e-05) * gain_ref[...]
        x = x.astype(jnp.bfloat16)
        top = jnp.full((tokens, 1), very_low, jnp.float32)
        total = jnp.zeros((tokens, 1), jnp.float32)
        summed = jnp.zeros((tokens, HEAD_WIDTH), jnp.float32)
        for zz in range(depth):
            keys = kv[zz, :, 0].reshape(chunk, HEAD_WIDTH)
            vals = kv[zz, :, 1].reshape(chunk, HEAD_WIDTH)
            scores = (
                lax.dot_general(
                    x, keys, (((1,), (1,)), ((), ())), preferred_element_type=jnp.float32
                )
                * scale
            )
            ids = zz * INNER + lax.broadcasted_iota(jnp.int32, (tokens, chunk), 1) // V_DEV
            allowed = (ids >= low) & (ids < high)
            masked = jnp.where(allowed, scores, very_low)
            newest = jnp.maximum(top, jnp.max(masked, axis=1, keepdims=True))
            weights = jnp.where(allowed, jnp.exp(masked - newest), 0.0)
            factor = jnp.exp(top - newest)
            total = total * factor + jnp.sum(weights, axis=1, keepdims=True)
            summed = summed * factor + jnp.dot(
                weights.astype(jnp.bfloat16), vals, preferred_element_type=jnp.float32
            )
            top = newest
        att[a, g, :, lanes] = (summed / total).astype(jnp.bfloat16)
        return carry

    lax.fori_loop(0, heads, one_head, 0)

    n_att = 0
    for dg in range(1, groups):
        send(
            att.at[a, g],
            att.at[a, g],
            att_send.at[n_att],
            att_recv.at[a, g],
            (f, (g + dg) % groups),
        )
        n_att += 1
    for dg in range(groups):
        gg = (g + dg) % groups
        if dg:
            arrived(att.at[a, gg], att_send.at[0], att_recv.at[a, gg])
        for aa in (a_x, a_c):
            send(
                att.at[a, gg],
                att.at[a, gg],
                att_send.at[n_att],
                att_recv.at[a, gg],
                (z * INNER + aa, g),
            )
            n_att += 1
    for dg in range(groups):
        gg = (g + dg) % groups
        arrived(att.at[a_x, gg], att_send.at[0], att_recv.at[a_x, gg])
        send(
            att.at[a_x, gg],
            att.at[a_x, gg],
            att_send.at[n_att],
            att_recv.at[a_x, gg],
            (z * INNER + a_c, g),
        )
        n_att += 1
    for dg in range(groups):
        gg = (g + dg) % groups
        for aa in (a_c, a_xc):
            arrived(att.at[aa, gg], att_send.at[0], att_recv.at[aa, gg])
    for dz in range(1, depth):
        zz = (z + dz) % depth
        for dg in range(groups):
            gg = (g + dg) % groups
            arrived(wbuf.at[zz, gg], wz_send.at[0], wz_recv.at[zz, gg])

    gate = jnp.tanh(gate_ref[...])
    width = heads * HEAD_WIDTH
    for j in range(INNER):
        aa = (a + 1 + j) % INNER
        acc = jnp.zeros((tokens, cols), jnp.float32)
        for gg in range(groups):
            acc = acc + jnp.dot(
                att[aa, gg], wbuf[:, gg].reshape(width, cols), preferred_element_type=jnp.float32
            )
        done = (gate * acc).astype(jnp.bfloat16)
        mine = pl.ds(pl.multiple_of(a * cols, 128), cols)
        if j == INNER - 1:
            out_ref[:, mine] = done
        else:
            obuf[j] = done
            send(
                obuf.at[j],
                out_ref.at[:, mine],
                out_send.at[j],
                out_recv.at[a],
                (z * INNER + aa, g),
            )
    for da in range(1, INNER):
        aa = (a + da) % INNER
        there = pl.ds(pl.multiple_of(aa * cols, 128), cols)
        arrived(out_ref.at[:, there], out_send.at[0], out_recv.at[aa])
    for copy in pending:
        copy.wait_send()


def local(queries, keys, values, q_gain, frame_bounds, output_weight, attn_gate):
    frames = lax.axis_size("frame")
    groups = lax.axis_size("group")
    tokens, width = queries.shape
    rows = output_weight.shape[1]
    cols = output_weight.shape[2] // (groups * INNER)
    depth = frames // INNER
    dma = pltpu.SemaphoreType.DMA
    vmem = pl.BlockSpec(memory_space=pltpu.VMEM)
    plane = groups * INNER
    return pl.pallas_call(
        functools.partial(kernel, frames, groups),
        out_shape=jax.ShapeDtypeStruct((tokens, INNER * cols), jnp.bfloat16),
        in_specs=[vmem] * 7,
        out_specs=vmem,
        scratch_shapes=[
            pltpu.VMEM((depth, INNER, 2, keys.shape[0], HEAD_WIDTH), jnp.bfloat16),
            pltpu.VMEM((INNER, groups, tokens, width), jnp.bfloat16),
            pltpu.VMEM((depth, groups, INNER, rows, cols), jnp.bfloat16),
            pltpu.VMEM((INNER - 1, tokens, cols), jnp.bfloat16),
            dma((depth, INNER)),
            dma((4 * depth - 1,)),
            dma((groups, INNER)),
            dma((plane - 1,)),
            dma((depth, groups)),
            dma((groups * (depth - 1),)),
            dma((INNER, groups)),
            dma((4 * groups - 1,)),
            dma((INNER,)),
            dma((INNER - 1,)),
            dma(()),
        ],
        compiler_params=pltpu.CompilerParams(
            collective_id=0, has_side_effects=True, vmem_limit_bytes=48 * 1024 * 1024
        ),
        cost_estimate=pl.CostEstimate(
            flops=3 * 1024**3, bytes_accessed=4 * 1024**2, transcendentals=2 * 1024**2
        ),
    )(
        queries,
        keys,
        values,
        q_gain.reshape(1, HEAD_WIDTH),
        frame_bounds,
        output_weight,
        attn_gate.reshape(1, 1),
    )


def solution(mesh):
    placed = (
        P("frame", "group"),
        P("frame", "group"),
        P("frame", "group"),
        P(),
        P(None, "frame"),
        P("group", "frame", None),
        P(),
    )
    return jax.shard_map(
        local, mesh=mesh, in_specs=placed, out_specs=P("frame", "group"), check_vma=False
    )
```

time: 140 us -> 70.7 us (0.51)
  the two profiles are of different devices: /device:TPU:0 before, /device:TPU:29 now
where the time goes in v1:
time: 70.7 us; the launch traced here: 70.3 us
  Pallas kernels  64.7 us (92%)
  local copies, waits for them, and re-layouts  4.97 us (7%)
    pallas_call x1, Pallas kernels, local(): pl.pallas_call(functools.partial(kernel, frames, groups), out_shape=jax.S...  64.7 us
    unnamed x13, local copies, waits for them, and re-layouts  4.97 us

profile of v1, /device:TPU:29, one launch (start us, length us, event | category | flops | bytes accessed | tf_op | source)
XLA Modules:
  0.0 70.3 jit_solution(15576480970697260416)
XLA Ops:
  0.7 0.0 copy-start.4
  0.7 0.0 copy-start.5
  0.7 0.7 copy-done.4
  1.3 0.0 copy-done.5
  1.3 0.0 copy-start
  1.3 1.0 %copy-done = bf16[1,64,4096]{2,1,0:T(8,128)(2,1)S(1)} copy-done((bf16[1,64,4096]{2,1,0:T(8,128)(2,1)S(1)}, bf16[1,64,4096]{2,1,0:T(8,128)(2,1)}, u32[]{:S(2)}) %copy-start) | copy-done | bytes 524312
  2.4 0.0 copy-start.1
  2.4 0.9 %copy-done.1 = bf16[128,1024]{1,0:T(8,128)(2,1)S(1)} copy-done((bf16[128,1024]{1,0:T(8,128)(2,1)S(1)}, bf16[128,1024]{1,0:T(8,128)(2,1)}, u32[]{:S(2)}) %copy-start.1) | copy-done | bytes 262168
  3.3 0.0 copy-start.2
  3.3 0.8 %copy-done.2 = bf16[128,128]{1,0:T(8,128)(2,1)S(1)} copy-done((bf16[128,128]{1,0:T(8,128)(2,1)S(1)}, bf16[128,128]{1,0:T(8,128)(2,1)}, u32[]{:S(2)}) %copy-start.2) | copy-done | bytes 32792
  4.1 0.0 copy-start.3
  4.1 0.8 %copy-done.3 = bf16[128,128]{1,0:T(8,128)(2,1)S(1)} copy-done((bf16[128,128]{1,0:T(8,128)(2,1)S(1)}, bf16[128,128]{1,0:T(8,128)(2,1)}, u32[]{:S(2)}) %copy-start.3) | copy-done | bytes 32792
  4.8 64.7 %shard_map.73 = bf16[128,2048]{1,0:T(8,128)(2,1)S(1)} custom-call(bf16[128,1024]{1,0:T(8,128)(2,1)S(1)} %copy-done.1, bf16[128,128]{1,0:T(8,128)(2,1)S(1)} %copy-done.2, bf16[128,128]{1,0:T(8,128)(2,1)S(1)} %copy-done.3, f32[1,128]{1,0:T(1,128)S(1)} %bitcast.3, s32[2,128]{1,0:T(2,128)S(1)} %copy-done.4, bf16[1,64,4096]{2,1,0:T(8,128)(2,1)S(1)} %copy-done, ...), custom_call_target="tpu_custom_call" | custom-call | flops 3221225472 | bytes 4194304 | tf_op jit(solution)/shard_map/pallas_call | solution.py:310
  69.5 0.8 %copy.10 = bf16[128,2048]{1,0:T(8,128)(2,1)} copy(bf16[128,2048]{1,0:T(8,128)(2,1)S(1)} %shard_map.73) | data formatting | bytes 1048576
Async XLA Ops:
  0.7 0.7 copy-start.4
  0.7 0.7 copy-start.5
  1.3 1.0 %copy-start = (bf16[1,64,4096]{2,1,0:T(8,128)(2,1)S(1)}, bf16[1,64,4096]{2,1,0:T(8,128)(2,1)}, u32[]{:S(2)}) copy-start(bf16[1,64,4096]{2,1,0:T(8,128)(2,1)} %w_ref.1) | copy-start | bytes 1572868
  2.4 0.9 %copy-start.1 = (bf16[128,1024]{1,0:T(8,128)(2,1)S(1)}, bf16[128,1024]{1,0:T(8,128)(2,1)}, u32[]{:S(2)}) copy-start(bf16[128,1024]{1,0:T(8,128)(2,1)} %q_ref.1) | copy-start | bytes 786436
  3.3 0.8 %copy-start.2 = (bf16[128,128]{1,0:T(8,128)(2,1)S(1)}, bf16[128,128]{1,0:T(8,128)(2,1)}, u32[]{:S(2)}) copy-start(bf16[128,128]{1,0:T(8,128)(2,1)} %k_ref.1) | copy-start | bytes 98308
  4.1 0.8 %copy-start.3 = (bf16[128,128]{1,0:T(8,128)(2,1)S(1)}, bf16[128,128]{1,0:T(8,128)(2,1)}, u32[]{:S(2)}) copy-start(bf16[128,128]{1,0:T(8,128)(2,1)} %v_ref.1) | copy-start | bytes 98308

commit v2 on v1

--- a/solution.py
+++ b/solution.py
@@ -18,14 +18,17 @@
 def kernel(
     frames,
     groups,
-    q_ref,
-    k_ref,
-    v_ref,
-    gain_ref,
-    bounds_ref,
+    q_hbm,
+    k_hbm,
+    v_hbm,
+    gain_hbm,
+    bounds_hbm,
     w_ref,
     gate_ref,
     out_ref,
+    q_ref,
+    gain_ref,
+    bounds_ref,
     kv,
     att,
     wbuf,
@@ -41,9 +44,12 @@
     out_recv,
     out_send,
     own_sem,
+    in_sem,
 ):
     depth = frames // INNER
-    cols = wbuf.shape[4]
+    halves = wbuf.shape[0]
+    half = wbuf.shape[5]
+    cols = halves * half
     tokens = q_ref.shape[0]
     heads = q_ref.shape[1] // HEAD_WIDTH
     f = lax.axis_index("frame")
@@ -58,10 +64,10 @@
 
     barrier = pltpu.get_barrier_semaphore()
     greeted = 0
-    for step in range(1, frames):
-        pl.semaphore_signal(
-            barrier, inc=1, device_id=((f + step) % frames, g), device_id_type=MESH
-        )
+    others = [((z + dz) % depth * INNER + a, g) for dz in range(1, depth)]
+    others += [(z * INNER + (a + da) % INNER, g) for da in range(1, INNER)]
+    for other in others:
+        pl.semaphore_signal(barrier, inc=1, device_id=other, device_id_type=MESH)
         greeted += 1
     for dg in range(1, groups):
         for da in range(INNER):
@@ -72,11 +78,26 @@
                 device_id_type=MESH,
             )
             greeted += 1
-    kv[z, a, 0] = k_ref[...]
-    kv[z, a, 1] = v_ref[...]
+    brought = [
+        pltpu.make_async_copy(source, target, in_sem.at[i])
+        for i, (source, target) in enumerate(
+            (
+                (k_hbm, kv.at[z, a, 0]),
+                (v_hbm, kv.at[z, a, 1]),
+                (q_hbm, q_ref),
+                (gain_hbm, gain_ref),
+                (bounds_hbm, bounds_ref),
+            )
+        )
+    ]
+    for copy in brought:
+        copy.start()
+    brought[0].wait()
+    brought[1].wait()
     pl.semaphore_wait(barrier, greeted)
 
     pending = []
+    pending_if = []
 
     def send(src, dst, send_sem, recv_sem, to):
         copy = pltpu.make_async_remote_copy(
@@ -111,26 +132,33 @@
         )
         n_kv += 1
 
-    def columns(ga, aa):
-        return pl.ds(pl.multiple_of((ga * INNER + aa) * cols, 128), cols)
-
-    own = pltpu.make_async_copy(w_ref.at[0, :, columns(g, a)], wbuf.at[z, g, a], own_sem)
-    own.start()
+    def columns(ga, aa, part):
+        start = (ga * INNER + aa) * cols + part * half
+        return pl.ds(pl.multiple_of(start, half), half)
+
+    own = [
+        pltpu.make_async_copy(
+            w_ref.at[0, :, columns(g, a, part)], wbuf.at[part, z, g, a], own_sem.at[part]
+        )
+        for part in range(halves)
+    ]
     n_w = 0
-    for dg in range(groups):
-        for da in range(INNER):
-            if dg == 0 and da == 0:
-                continue
-            gg = (g + dg) % groups
-            aa = (a + da) % INNER
-            send(
-                w_ref.at[0, :, columns(gg, aa)],
-                wbuf.at[z, g, a],
-                w_send.at[n_w],
-                w_recv.at[g, a],
-                (z * INNER + aa, gg),
-            )
-            n_w += 1
+    for part in range(halves):
+        own[part].start()
+        for dg in range(groups):
+            for da in range(INNER):
+                if dg == 0 and da == 0:
+                    continue
+                gg = (g + dg) % groups
+                aa = (a + da) % INNER
+                send(
+                    w_ref.at[0, :, columns(gg, aa, part)],
+                    wbuf.at[part, z, g, a],
+                    w_send.at[n_w],
+                    w_recv.at[part, g, a],
+                    (z * INNER + aa, gg),
+                )
+                n_w += 1
 
     for dz in range(depth):
         zz = (z + dz) % depth
@@ -146,24 +174,49 @@
             )
             n_kv += 1
 
-    own.wait()
-    n_wz = 0
-    for dg in range(groups):
-        gg = (g + dg) % groups
-        for da in range(INNER):
-            if dg == 0 and da == 0:
-                continue
-            aa = (a + da) % INNER
-            arrived(wbuf.at[z, gg, aa], w_send.at[0], w_recv.at[gg, aa])
-        for dz in range(1, depth):
-            send(
-                wbuf.at[z, gg],
-                wbuf.at[z, gg],
-                wz_send.at[n_wz],
-                wz_recv.at[z, gg],
-                ((z + dz) % depth * INNER + a, g),
-            )
-            n_wz += 1
+    def pass_on(block, part, to, exists, way, hop):
+        copy = pltpu.make_async_remote_copy(
+            src_ref=wbuf.at[part, block],
+            dst_ref=wbuf.at[part, block],
+            send_sem=wz_send.at[way, hop, part],
+            recv_sem=wz_recv.at[block, part],
+            device_id=(to * INNER + a, g),
+            device_id_type=MESH,
+        )
+        pending_if.append((exists, copy))
+        return copy
+
+    def below_above(hop, part):
+        below = z - hop
+        above = z + hop
+        for block, to, way in ((below, z + 1, 0), (above, z - 1, 1)):
+            here = block >= 0 if way == 0 else block < depth
+            onward = to < depth if way == 0 else to >= 0
+            at = lax.clamp(0, block, depth - 1)
+            exists = jnp.logical_and(here, onward)
+            if hop:
+
+                @pl.when(here)
+                def _():
+                    arrived(wbuf.at[part, at], wz_send.at[0, 0, 0], wz_recv.at[at, part])
+
+            if hop < depth - 1:
+                copy = pass_on(at, part, lax.clamp(0, to, depth - 1), exists, way, hop)
+
+                @pl.when(exists)
+                def _():
+                    copy.start()
+
+    for part in range(halves):
+        own[part].wait()
+        for dg in range(groups):
+            gg = (g + dg) % groups
+            for da in range(INNER):
+                if dg == 0 and da == 0:
+                    continue
+                aa = (a + da) % INNER
+                arrived(wbuf.at[part, z, gg, aa], w_send.at[0], w_recv.at[part, gg, aa])
+        below_above(0, part)
 
     for dz in range(depth):
         zz = (z + dz) % depth
@@ -180,6 +233,9 @@
         zz = (z + dz) % depth
         for aa in (a_c, a_xc):
             arrived(kv.at[zz, aa], kv_send.at[0], kv_recv.at[zz, aa])
+
+    for copy in brought[2:]:
+        copy.wait()
 
     def spread(row):
         wide = jnp.broadcast_to(bounds_ref[row : row + 1, :].astype(jnp.float32), (tokens, tokens))
@@ -221,7 +277,9 @@
         att[a, g, :, lanes] = (summed / total).astype(jnp.bfloat16)
         return carry
 
-    lax.fori_loop(0, heads, one_head, 0)
+    lax.fori_loop(0, heads // 2, one_head, 0)
+    below_above(1, 0)
+    lax.fori_loop(heads // 2, heads, one_head, 0)
 
     n_att = 0
     for dg in range(1, groups):
@@ -233,6 +291,8 @@
             (f, (g + dg) % groups),
         )
         n_att += 1
+    for hop in range(2, depth - 1):
+        below_above(hop, 0)
     for dg in range(groups):
         gg = (g + dg) % groups
         if dg:
@@ -246,6 +306,9 @@
                 (z * INNER + aa, g),
             )
             n_att += 1
+    for part in range(1, halves):
+        for hop in range(1, depth - 1):
+            below_above(hop, part)
     for dg in range(groups):
         gg = (g + dg) % groups
         arrived(att.at[a_x, gg], att_send.at[0], att_recv.at[a_x, gg])
@@ -261,40 +324,45 @@
         gg = (g + dg) % groups
         for aa in (a_c, a_xc):
             arrived(att.at[aa, gg], att_send.at[0], att_recv.at[aa, gg])
-    for dz in range(1, depth):
-        zz = (z + dz) % depth
-        for dg in range(groups):
-            gg = (g + dg) % groups
-            arrived(wbuf.at[zz, gg], wz_send.at[0], wz_recv.at[zz, gg])
 
     gate = jnp.tanh(gate_ref[...])
     width = heads * HEAD_WIDTH
-    for j in range(INNER):
-        aa = (a + 1 + j) % INNER
-        acc = jnp.zeros((tokens, cols), jnp.float32)
+
+    def target(aa, part):
+        return pl.ds(pl.multiple_of(aa * cols + part * half, half), half)
+
+    for part in range(halves):
+        below_above(depth - 1, part)
+        acc = jnp.zeros((INNER * tokens, half), jnp.float32)
         for gg in range(groups):
             acc = acc + jnp.dot(
-                att[aa, gg], wbuf[:, gg].reshape(width, cols), preferred_element_type=jnp.float32
+                att[:, gg].reshape(INNER * tokens, width),
+                wbuf[part, :, gg].reshape(width, half),
+                preferred_element_type=jnp.float32,
             )
         done = (gate * acc).astype(jnp.bfloat16)
-        mine = pl.ds(pl.multiple_of(a * cols, 128), cols)
-        if j == INNER - 1:
-            out_ref[:, mine] = done
-        else:
-            obuf[j] = done
+        obuf[part] = done.reshape(INNER, tokens, half)
+        for da in (2, 3, 1):
+            aa = (a + da) % INNER
             send(
-                obuf.at[j],
-                out_ref.at[:, mine],
-                out_send.at[j],
-                out_recv.at[a],
+                obuf.at[part, aa],
+                out_ref.at[:, target(a, part)],
+                out_send.at[part, da - 1],
+                out_recv.at[part, a],
                 (z * INNER + aa, g),
             )
-    for da in range(1, INNER):
-        aa = (a + da) % INNER
-        there = pl.ds(pl.multiple_of(aa * cols, 128), cols)
-        arrived(out_ref.at[:, there], out_send.at[0], out_recv.at[aa])
+        out_ref[:, target(a, part)] = obuf[part, a]
+    for part in range(halves):
+        for da in range(1, INNER):
+            aa = (a + da) % INNER
+            arrived(out_ref.at[:, target(aa, part)], out_send.at[0, 0], out_recv.at[part, aa])
     for copy in pending:
         copy.wait_send()
+    for exists, copy in pending_if:
+
+        @pl.when(exists)
+        def _():
+            copy.wait_send()
 
 
 def local(queries, keys, values, q_gain, frame_bounds, output_weight, attn_gate):
@@ -307,30 +375,37 @@
     dma = pltpu.SemaphoreType.DMA
     vmem = pl.BlockSpec(memory_space=pltpu.VMEM)
     plane = groups * INNER
+    halves = 2 if cols % 256 == 0 else 1
+    half = cols // halves
+    anywhere = pl.BlockSpec(memory_space=pl.ANY)
     return pl.pallas_call(
         functools.partial(kernel, frames, groups),
         out_shape=jax.ShapeDtypeStruct((tokens, INNER * cols), jnp.bfloat16),
-        in_specs=[vmem] * 7,
+        in_specs=[anywhere] * 6 + [vmem],
         out_specs=vmem,
         scratch_shapes=[
+            pltpu.VMEM((tokens, width), jnp.bfloat16),
+            pltpu.VMEM((1, HEAD_WIDTH), jnp.float32),
+            pltpu.VMEM((2, tokens), jnp.int32),
             pltpu.VMEM((depth, INNER, 2, keys.shape[0], HEAD_WIDTH), jnp.bfloat16),
             pltpu.VMEM((INNER, groups, tokens, width), jnp.bfloat16),
-            pltpu.VMEM((depth, groups, INNER, rows, cols), jnp.bfloat16),
-            pltpu.VMEM((INNER - 1, tokens, cols), jnp.bfloat16),
+            pltpu.VMEM((halves, depth, groups, INNER, rows, half), jnp.bfloat16),
+            pltpu.VMEM((halves, INNER, tokens, half), jnp.bfloat16),
             dma((depth, INNER)),
             dma((4 * depth - 1,)),
-            dma((groups, INNER)),
-            dma((plane - 1,)),
-            dma((depth, groups)),
-            dma((groups * (depth - 1),)),
+            dma((halves, groups, INNER)),
+            dma((halves * (plane - 1),)),
+            dma((depth, halves)),
+            dma((2, depth - 1, halves)),
             dma((INNER, groups)),
             dma((4 * groups - 1,)),
-            dma((INNER,)),
-            dma((INNER - 1,)),
-            dma(()),
+            dma((halves, INNER)),
+            dma((halves, INNER - 1)),
+            dma((halves,)),
+            dma((5,)),
         ],
         compiler_params=pltpu.CompilerParams(
-            collective_id=0, has_side_effects=True, vmem_limit_bytes=48 * 1024 * 1024
+            collective_id=0, has_side_effects=True, vmem_limit_bytes=60 * 1024 * 1024
         ),
         cost_estimate=pl.CostEstimate(
             flops=3 * 1024**3, bytes_accessed=4 * 1024**2, transcendentals=2 * 1024**2

time: 70.7 us -> 62.6 us (0.89)
  the two profiles are of different devices: /device:TPU:29 before, /device:TPU:0 now
where the time goes in v2:
time: 62.6 us; the launch traced here: 62.3 us
  Pallas kernels  59.8 us (96%)
  local copies, waits for them, and re-layouts  1.88 us (3%)
  between operations  0.66 us (1%)
    pallas_call x1, Pallas kernels, local(): pl.pallas_call(functools.partial(kernel, frames, groups), out_shape=jax.S...  59.8 us
    unnamed x1, local copies, waits for them, and re-layouts  1.88 us

profile of v2, /device:TPU:0, one launch (start us, length us, event | category | flops | bytes accessed | tf_op | source)
XLA Modules:
  0.0 62.3 jit_solution(7146879712590850010)
XLA Ops:
  0.7 59.8 %shard_map.73 = bf16[128,2048]{1,0:T(8,128)(2,1)} custom-call(bf16[128,1024]{1,0:T(8,128)(2,1)} %q_hbm.1, bf16[128,128]{1,0:T(8,128)(2,1)} %k_hbm.1, bf16[128,128]{1,0:T(8,128)(2,1)} %v_hbm.1, f32[1,128]{1,0:T(1,128)} %bitcast.3, s32[2,128]{1,0:T(2,128)} %bounds_hbm.1, bf16[1,64,4096]{2,1,0:T(8,128)(2,1)} %w_ref.1, f32[1,1]{1,0:T(1,128)} %bitcast.2.gate_ref), custom_call_target="tpu_custom_call" | custom-call | flops 3221225472 | bytes 4194304 | tf_op jit(solution)/shard_map/pallas_call | solution.py:381
  60.4 1.9 %copy.10 = bf16[128,2048]{1,0:T(8,128)(2,1)} copy(bf16[128,2048]{1,0:T(8,128)(2,1)} %shard_map.73) | data formatting | bytes 1048576

commit v3 on v2

--- a/solution.py
+++ b/solution.py
@@ -29,6 +29,8 @@
     q_ref,
     gain_ref,
     bounds_ref,
+    bias,
+    logits,
     kv,
     att,
     wbuf,
@@ -50,6 +52,7 @@
     halves = wbuf.shape[0]
     half = wbuf.shape[5]
     cols = halves * half
+    parts = att.shape[0]
     tokens = q_ref.shape[0]
     heads = q_ref.shape[1] // HEAD_WIDTH
     f = lax.axis_index("frame")
@@ -160,6 +163,67 @@
                 )
                 n_w += 1
 
+    for copy in brought[2:]:
+        copy.wait()
+
+    def spread(row):
+        wide = jnp.broadcast_to(
+            bounds_ref[row : row + 1, :].astype(jnp.float32), (V_DEV, tokens)
+        )
+        return wide.T
+
+    low = spread(0)
+    high = spread(1)
+    for block in range(frames):
+        allowed = (low <= block) & (high > block)
+        bias[:, block * V_DEV : (block + 1) * V_DEV] = jnp.where(allowed, 0.0, very_low)
+
+    def pass_on(block, part, to, exists, way, hop):
+        copy = pltpu.make_async_remote_copy(
+            src_ref=wbuf.at[part, block],
+            dst_ref=wbuf.at[part, block],
+            send_sem=wz_send.at[way, hop, part],
+            recv_sem=wz_recv.at[block, part],
+            device_id=(to * INNER + a, g),
+            device_id_type=MESH,
+        )
+        pending_if.append((exists, copy))
+        return copy
+
+    def below_above(hop, part):
+        below = z - hop
+        above = z + hop
+        for block, to, way in ((below, z + 1, 0), (above, z - 1, 1)):
+            here = block >= 0 if way == 0 else block < depth
+            onward = to < depth if way == 0 else to >= 0
+            at = lax.clamp(0, block, depth - 1)
+            exists = jnp.logical_and(here, onward)
+            if hop:
+
+                @pl.when(here)
+                def _():
+                    arrived(wbuf.at[part, at], wz_send.at[0, 0, 0], wz_recv.at[at, part])
+
+            if hop < depth - 1:
+                copy = pass_on(at, part, lax.clamp(0, to, depth - 1), exists, way, hop)
+
+                @pl.when(exists)
+                def _():
+                    copy.start()
+
+    def begin(part):
+        own[part].wait()
+        for dg in range(groups):
+            gg = (g + dg) % groups
+            for da in range(INNER):
+                if dg == 0 and da == 0:
+                    continue
+                aa = (a + da) % INNER
+                arrived(wbuf.at[part, z, gg, aa], w_send.at[0], w_recv.at[part, gg, aa])
+        below_above(0, part)
+
+    begin(0)
+
     for dz in range(depth):
         zz = (z + dz) % depth
         if dz:
@@ -174,49 +238,8 @@
             )
             n_kv += 1
 
-    def pass_on(block, part, to, exists, way, hop):
-        copy = pltpu.make_async_remote_copy(
-            src_ref=wbuf.at[part, block],
-            dst_ref=wbuf.at[part, block],
-            send_sem=wz_send.at[way, hop, part],
-            recv_sem=wz_recv.at[block, part],
-            device_id=(to * INNER + a, g),
-            device_id_type=MESH,
-        )
-        pending_if.append((exists, copy))
-        return copy
-
-    def below_above(hop, part):
-        below = z - hop
-        above = z + hop
-        for block, to, way in ((below, z + 1, 0), (above, z - 1, 1)):
-            here = block >= 0 if way == 0 else block < depth
-            onward = to < depth if way == 0 else to >= 0
-            at = lax.clamp(0, block, depth - 1)
-            exists = jnp.logical_and(here, onward)
-            if hop:
-
-                @pl.when(here)
-                def _():
-                    arrived(wbuf.at[part, at], wz_send.at[0, 0, 0], wz_recv.at[at, part])
-
-            if hop < depth - 1:
-                copy = pass_on(at, part, lax.clamp(0, to, depth - 1), exists, way, hop)
-
-                @pl.when(exists)
-                def _():
-                    copy.start()
-
-    for part in range(halves):
-        own[part].wait()
-        for dg in range(groups):
-            gg = (g + dg) % groups
-            for da in range(INNER):
-                if dg == 0 and da == 0:
-                    continue
-                aa = (a + da) % INNER
-                arrived(wbuf.at[part, z, gg, aa], w_send.at[0], w_recv.at[part, gg, aa])
-        below_above(0, part)
+    for part in range(1, halves):
+        begin(part)
 
     for dz in range(depth):
         zz = (z + dz) % depth
@@ -234,96 +257,92 @@
         for aa in (a_c, a_xc):
             arrived(kv.at[zz, aa], kv_send.at[0], kv_recv.at[zz, aa])
 
-    for copy in brought[2:]:
-        copy.wait()
-
-    def spread(row):
-        wide = jnp.broadcast_to(bounds_ref[row : row + 1, :].astype(jnp.float32), (tokens, tokens))
-        return wide.T[:, :1].astype(jnp.int32)
-
-    low = spread(0)
-    high = spread(1)
-    scale = 1.0 / math.sqrt(HEAD_WIDTH)
-    chunk = INNER * V_DEV
-
-    def one_head(h, carry):
-        lanes = pl.ds(pl.multiple_of(h * HEAD_WIDTH, HEAD_WIDTH), HEAD_WIDTH)
-        x = q_ref[:, lanes].astype(jnp.float32)
-        x = x * lax.rsqrt(jnp.mean(x * x, axis=-1, keepdims=True) + 1e-05) * gain_ref[...]
-        x = x.astype(jnp.bfloat16)
-        top = jnp.full((tokens, 1), very_low, jnp.float32)
-        total = jnp.zeros((tokens, 1), jnp.float32)
-        summed = jnp.zeros((tokens, HEAD_WIDTH), jnp.float32)
-        for zz in range(depth):
-            keys = kv[zz, :, 0].reshape(chunk, HEAD_WIDTH)
-            vals = kv[zz, :, 1].reshape(chunk, HEAD_WIDTH)
-            scores = (
-                lax.dot_general(
-                    x, keys, (((1,), (1,)), ((), ())), preferred_element_type=jnp.float32
-                )
-                * scale
-            )
-            ids = zz * INNER + lax.broadcasted_iota(jnp.int32, (tokens, chunk), 1) // V_DEV
-            allowed = (ids >= low) & (ids < high)
-            masked = jnp.where(allowed, scores, very_low)
-            newest = jnp.maximum(top, jnp.max(masked, axis=1, keepdims=True))
-            weights = jnp.where(allowed, jnp.exp(masked - newest), 0.0)
-            factor = jnp.exp(top - newest)
-            total = total * factor + jnp.sum(weights, axis=1, keepdims=True)
-            summed = summed * factor + jnp.dot(
+    fold = math.log2(math.e) / math.sqrt(HEAD_WIDTH)
+    per = heads // parts
+    rows = per * tokens
+    pair = 2 * V_DEV
+
+    def attend(part):
+        normed = []
+        for h in range(part * per, (part + 1) * per):
+            x = q_ref[:, h * HEAD_WIDTH : (h + 1) * HEAD_WIDTH].astype(jnp.float32)
+            x = x * lax.rsqrt(jnp.mean(x * x, axis=-1, keepdims=True) + 1e-05) * gain_ref[...]
+            normed.append(x.astype(jnp.bfloat16))
+        x = jnp.concatenate(normed, axis=0)
+        top = jnp.full((rows, V_DEV), very_low, jnp.float32)
+        for n in range(frames // 2):
+            at = n * 2 // INNER
+            first = n * 2 % INNER
+            keys = kv[at, first : first + 2, 0].reshape(pair, HEAD_WIDTH)
+            scores = lax.dot_general(
+                x, keys, (((1,), (1,)), ((), ())), preferred_element_type=jnp.float32
+            )
+            offset = bias[:, n * pair : (n + 1) * pair]
+            scores = scores * fold + jnp.concatenate([offset] * per, axis=0)
+            logits[:, n * pair : (n + 1) * pair] = scores
+            top = jnp.maximum(top, jnp.maximum(scores[:, :V_DEV], scores[:, V_DEV:]))
+        top = jnp.max(top, axis=1, keepdims=True)
+        total = jnp.zeros((rows, V_DEV), jnp.float32)
+        summed = jnp.zeros((rows, HEAD_WIDTH), jnp.float32)
+        for n in range(frames // 2):
+            at = n * 2 // INNER
+            first = n * 2 % INNER
+            vals = kv[at, first : first + 2, 1].reshape(pair, HEAD_WIDTH)
+            weights = jnp.exp2(logits[:, n * pair : (n + 1) * pair] - top)
+            total = total + (weights[:, :V_DEV] + weights[:, V_DEV:])
+            summed = summed + jnp.dot(
                 weights.astype(jnp.bfloat16), vals, preferred_element_type=jnp.float32
             )
-            top = newest
-        att[a, g, :, lanes] = (summed / total).astype(jnp.bfloat16)
-        return carry
-
-    lax.fori_loop(0, heads // 2, one_head, 0)
-    below_above(1, 0)
-    lax.fori_loop(heads // 2, heads, one_head, 0)
-
-    n_att = 0
-    for dg in range(1, groups):
+        total = jnp.sum(total, axis=1, keepdims=True)
+        result = (summed / total).astype(jnp.bfloat16)
+        for h in range(per):
+            att[part, a, g, :, h * HEAD_WIDTH : (h + 1) * HEAD_WIDTH] = result[
+                h * tokens : (h + 1) * tokens
+            ]
+
+    n_att = [0]
+
+    def hand(part, aa, gg, to):
         send(
-            att.at[a, g],
-            att.at[a, g],
-            att_send.at[n_att],
-            att_recv.at[a, g],
-            (f, (g + dg) % groups),
-        )
-        n_att += 1
-    for hop in range(2, depth - 1):
-        below_above(hop, 0)
-    for dg in range(groups):
-        gg = (g + dg) % groups
-        if dg:
-            arrived(att.at[a, gg], att_send.at[0], att_recv.at[a, gg])
-        for aa in (a_x, a_c):
-            send(
-                att.at[a, gg],
-                att.at[a, gg],
-                att_send.at[n_att],
-                att_recv.at[a, gg],
-                (z * INNER + aa, g),
-            )
-            n_att += 1
-    for part in range(1, halves):
-        for hop in range(1, depth - 1):
+            att.at[part, aa, gg],
+            att.at[part, aa, gg],
+            att_send.at[n_att[0]],
+            att_recv.at[part, aa, gg],
+            to,
+        )
+        n_att[0] += 1
+
+    def await_att(part, aa, gg):
+        arrived(att.at[part, aa, gg], att_send.at[0], att_recv.at[part, aa, gg])
+
+    tasks = [(hop, part) for hop in range(1, depth - 1) for part in range(halves)]
+    steps = parts + 2
+    for step in range(steps):
+        if step < parts:
+            attend(step)
+        for hop, part in tasks[-(-step * len(tasks) // steps) : -(-(step + 1) * len(tasks) // steps)]:
             below_above(hop, part)
-    for dg in range(groups):
-        gg = (g + dg) % groups
-        arrived(att.at[a_x, gg], att_send.at[0], att_recv.at[a_x, gg])
-        send(
-            att.at[a_x, gg],
-            att.at[a_x, gg],
-            att_send.at[n_att],
-            att_recv.at[a_x, gg],
-            (z * INNER + a_c, g),
-        )
-        n_att += 1
-    for dg in range(groups):
-        gg = (g + dg) % groups
-        for aa in (a_c, a_xc):
-            arrived(att.at[aa, gg], att_send.at[0], att_recv.at[aa, gg])
+        if step < parts:
+            for dg in range(1, groups):
+                hand(step, a, g, (f, (g + dg) % groups))
+            for aa in (a_x, a_c):
+                hand(step, a, g, (z * INNER + aa, g))
+        if 1 <= step <= parts:
+            for dg in range(1, groups):
+                gg = (g + dg) % groups
+                await_att(step - 1, a, gg)
+                for aa in (a_x, a_c):
+                    hand(step - 1, a, gg, (z * INNER + aa, g))
+        if step >= 2:
+            for dg in range(groups):
+                gg = (g + dg) % groups
+                await_att(step - 2, a_x, gg)
+                hand(step - 2, a_x, gg, (z * INNER + a_c, g))
+    for part in range(parts):
+        for dg in range(groups):
+            gg = (g + dg) % groups
+            for aa in (a_c, a_xc):
+                await_att(part, aa, gg)
 
     gate = jnp.tanh(gate_ref[...])
     width = heads * HEAD_WIDTH
@@ -335,11 +354,13 @@
         below_above(depth - 1, part)
         acc = jnp.zeros((INNER * tokens, half), jnp.float32)
         for gg in range(groups):
-            acc = acc + jnp.dot(
-                att[:, gg].reshape(INNER * tokens, width),
-                wbuf[part, :, gg].reshape(width, half),
-                preferred_element_type=jnp.float32,
-            )
+            weight = wbuf[part, :, gg].reshape(width, half)
+            for p in range(parts):
+                acc = acc + jnp.dot(
+                    att[p, :, gg].reshape(INNER * tokens, width // parts),
+                    weight[p * (width // parts) : (p + 1) * (width // parts)],
+                    preferred_element_type=jnp.float32,
+                )
         done = (gate * acc).astype(jnp.bfloat16)
         obuf[part] = done.reshape(INNER, tokens, half)
         for da in (2, 3, 1):
@@ -375,7 +396,10 @@
     dma = pltpu.SemaphoreType.DMA
     vmem = pl.BlockSpec(memory_space=pltpu.VMEM)
     plane = groups * INNER
-    halves = 2 if cols % 256 == 0 else 1
+    heads = width // HEAD_WIDTH
+    parts = 4
+    per = heads // parts
+    halves = cols // 128
     half = cols // halves
     anywhere = pl.BlockSpec(memory_space=pl.ANY)
     return pl.pallas_call(
@@ -387,8 +411,10 @@
             pltpu.VMEM((tokens, width), jnp.bfloat16),
             pltpu.VMEM((1, HEAD_WIDTH), jnp.float32),
             pltpu.VMEM((2, tokens), jnp.int32),
+            pltpu.VMEM((tokens, frames * V_DEV), jnp.float32),
+            pltpu.VMEM((per * tokens, frames * V_DEV), jnp.float32),
             pltpu.VMEM((depth, INNER, 2, keys.shape[0], HEAD_WIDTH), jnp.bfloat16),
-            pltpu.VMEM((INNER, groups, tokens, width), jnp.bfloat16),
+            pltpu.VMEM((parts, INNER, groups, tokens, width // parts), jnp.bfloat16),
             pltpu.VMEM((halves, depth, groups, INNER, rows, half), jnp.bfloat16),
             pltpu.VMEM((halves, INNER, tokens, half), jnp.bfloat16),
             dma((depth, INNER)),
@@ -397,8 +423,8 @@
             dma((halves * (plane - 1),)),
             dma((depth, halves)),
             dma((2, depth - 1, halves)),
-            dma((INNER, groups)),
-            dma((4 * groups - 1,)),
+            dma((parts, INNER, groups)),
+            dma((parts * (4 * groups - 1),)),
             dma((halves, INNER)),
             dma((halves, INNER - 1)),
             dma((halves,)),

time: 62.6 us -> 55.4 us (0.88)
  Pallas kernels: 59.8 us -> 52.7 us
    pallas_call x1, Pallas kernels: 59.8 us -> 52.7 us  [local(): pl.pallas_call(functools.partial(kernel, frames, groups), out_shape=jax.S...]
where the time goes in v3:
time: 55.4 us; the launch traced here: 55.2 us
  Pallas kernels  52.7 us (95%)
  local copies, waits for them, and re-layouts  1.88 us (3%)
  between operations  0.66 us (1%)
    pallas_call x1, Pallas kernels, local(): pl.pallas_call(functools.partial(kernel, frames, groups), out_shape=jax.S...  52.7 us
    unnamed x1, local copies, waits for them, and re-layouts  1.88 us

profile of v3, /device:TPU:0, one launch (start us, length us, event | category | flops | bytes accessed | tf_op | source)
XLA Modules:
  0.0 55.2 jit_solution(8471879378365617550)
XLA Ops:
  0.7 52.7 %shard_map.73 = bf16[128,2048]{1,0:T(8,128)(2,1)} custom-call(bf16[128,1024]{1,0:T(8,128)(2,1)} %q_hbm.1, bf16[128,128]{1,0:T(8,128)(2,1)} %k_hbm.1, bf16[128,128]{1,0:T(8,128)(2,1)} %v_hbm.1, f32[1,128]{1,0:T(1,128)} %bitcast.3, s32[2,128]{1,0:T(2,128)} %bounds_hbm.1, bf16[1,64,4096]{2,1,0:T(8,128)(2,1)} %w_ref.1, f32[1,1]{1,0:T(1,128)} %bitcast.2.gate_ref), custom_call_target="tpu_custom_call" | custom-call | flops 3221225472 | bytes 4194304 | tf_op jit(solution)/shard_map/pallas_call | solution.py:405
  53.3 1.9 %copy.10 = bf16[128,2048]{1,0:T(8,128)(2,1)} copy(bf16[128,2048]{1,0:T(8,128)(2,1)} %shard_map.73) | data formatting | bytes 1048576

commit v4 on v3

--- a/solution.py
+++ b/solution.py
@@ -163,21 +163,6 @@
                 )
                 n_w += 1
 
-    for copy in brought[2:]:
-        copy.wait()
-
-    def spread(row):
-        wide = jnp.broadcast_to(
-            bounds_ref[row : row + 1, :].astype(jnp.float32), (V_DEV, tokens)
-        )
-        return wide.T
-
-    low = spread(0)
-    high = spread(1)
-    for block in range(frames):
-        allowed = (low <= block) & (high > block)
-        bias[:, block * V_DEV : (block + 1) * V_DEV] = jnp.where(allowed, 0.0, very_low)
-
     def pass_on(block, part, to, exists, way, hop):
         copy = pltpu.make_async_remote_copy(
             src_ref=wbuf.at[part, block],
@@ -240,6 +225,21 @@
 
     for part in range(1, halves):
         begin(part)
+
+    for copy in brought[2:]:
+        copy.wait()
+
+    def spread(row):
+        wide = jnp.broadcast_to(
+            bounds_ref[row : row + 1, :].astype(jnp.float32), (V_DEV, tokens)
+        )
+        return wide.T
+
+    low = spread(0)
+    high = spread(1)
+    for block in range(frames):
+        allowed = (low <= block) & (high > block)
+        bias[:, block * V_DEV : (block + 1) * V_DEV] = jnp.where(allowed, 0.0, very_low)
 
     for dz in range(depth):
         zz = (z + dz) % depth

time: 55.4 us -> 55.4 us (level)
  no operation moved by 1% of the time
where the time goes in v4:
time: 55.4 us; the launch traced here: 55.2 us
  Pallas kernels  52.7 us (95%)
  local copies, waits for them, and re-layouts  1.88 us (3%)
  between operations  0.66 us (1%)
    pallas_call x1, Pallas kernels, local(): pl.pallas_call(functools.partial(kernel, frames, groups), out_shape=jax.S...  52.7 us
    unnamed x1, local copies, waits for them, and re-layouts  1.88 us

profile of v4, /device:TPU:0, one launch (start us, length us, event | category | flops | bytes accessed | tf_op | source)
XLA Modules:
  0.0 55.2 jit_solution(7781685119619929062)
XLA Ops:
  0.7 52.7 %shard_map.73 = bf16[128,2048]{1,0:T(8,128)(2,1)} custom-call(bf16[128,1024]{1,0:T(8,128)(2,1)} %q_hbm.1, bf16[128,128]{1,0:T(8,128)(2,1)} %k_hbm.1, bf16[128,128]{1,0:T(8,128)(2,1)} %v_hbm.1, f32[1,128]{1,0:T(1,128)} %bitcast.3, s32[2,128]{1,0:T(2,128)} %bounds_hbm.1, bf16[1,64,4096]{2,1,0:T(8,128)(2,1)} %w_ref.1, f32[1,1]{1,0:T(1,128)} %bitcast.2.gate_ref), custom_call_target="tpu_custom_call" | custom-call | flops 3221225472 | bytes 4194304 | tf_op jit(solution)/shard_map/pallas_call | solution.py:405
  53.3 1.9 %copy.10 = bf16[128,2048]{1,0:T(8,128)(2,1)} copy(bf16[128,2048]{1,0:T(8,128)(2,1)} %shard_map.73) | data formatting | bytes 1048576
